TPU v7x, 128 devices: a whole 4x4x4 slice. The times are simulated.
128 devices in a mesh: seq: 16 (over y, x), tp: 8 (over z, core).
Axes of the slice: x: 4, y: 4, z: 4, core: 2. Of those that a mesh axis runs over, the one named last changes fastest.
Arguments:
- hidden: bfloat16 [16384, 4096], P('seq'), may hold values from -6 to 6
- query_weight: bfloat16 [4096, 4096], P(None, 'tp'), may hold values from -0.09375 to 0.09375
- out_weight: bfloat16 [4096, 4096], P('tp'), may hold values from -0.75 to 0.75
- kv_cache: bfloat16 [128, 2, 128, 4096], P('seq', None, None, 'tp'), may hold values from -520 to 520
- nbr_shard: int32 [256, 2], P('seq'), may hold values from 0 to 15, all different within a row; in each aligned block of 16 rows (0 to 15, 16 to 31, ...) at most 4 rows name the same one
- nbr_row: int32 [256, 2], P('seq'), may hold values from 0 to 7
- nbr_count: int32 [256], P('seq'), may hold values from 1 to 2
Outputs:
- cca_out: bfloat16 [16384, 4096], P(('seq', 'tp'))
Inputs may be any that keep to these rules, and one draw needn't show every extreme that they name: `nbr_shard`: in each aligned block of 16 spans (the spans of one index of seq) no shard is named more than 4 times, and the 2 neighbours of a span lie on different shards.
All inputs are finite; a program needn't handle non-finite values.
Results may differ from a plain program's by a relative error of at most 0.02.
Values may be sent and summed in bfloat16 or wider, within the bound.
A program may use at most 192 MiB of HBM per device.

v0:
```python
import jax
import jax.numpy as jnp
from jax import lax
from jax.sharding import PartitionSpec as P

HEAD = 128
SPAN = 64
NBR = 2


def passed_along(shard, axis, by):
    devices = lax.axis_size(axis)
    pairs = [(i, i + by) for i in range(devices) if 0 <= i + by < devices]
    return lax.ppermute(shard, axis, pairs)


def partial_attend(query_blocks, key_rows, value_rows):
    pairs = query_blocks.shape[0]
    group_len = query_blocks.shape[1]
    local_width = query_blocks.shape[2]
    heads_here = local_width // HEAD
    query_split = query_blocks.reshape(pairs, group_len, heads_here, HEAD)
    key_split = key_rows.reshape(pairs, key_rows.shape[1], heads_here, HEAD)
    value_split = value_rows.reshape(pairs, value_rows.shape[1], heads_here, HEAD)
    scores = jnp.einsum(
        "bqhd,bkhd->bhqk", query_split, key_split, preferred_element_type=jnp.float32
    ) * HEAD ** (-0.5)
    highest = jnp.max(scores, axis=3)
    expon = jnp.exp(scores - highest[..., None])
    total = jnp.sum(expon, axis=3)
    weights = (expon / total[..., None]).astype(jnp.bfloat16)
    part = jnp.einsum("bhqk,bkhd->bqhd", weights, value_split, preferred_element_type=jnp.float32)
    return (part.astype(jnp.bfloat16).reshape(pairs, group_len, local_width), highest, total)


def combine(part, highest, total, counts):
    groups_here = counts.shape[0]
    group_len = part.shape[1]
    local_width = part.shape[2]
    heads_here = local_width // HEAD
    part = part.reshape(groups_here, NBR, group_len, heads_here, HEAD)
    highest = highest.reshape(groups_here, NBR, heads_here, group_len)
    total = total.reshape(groups_here, NBR, heads_here, group_len)
    used = (jnp.arange(NBR)[None, :] < jnp.maximum(counts, 1)[:, None])[:, :, None, None]
    top = jnp.max(jnp.where(used, highest, -1e30), axis=1, keepdims=True)
    safe = jnp.where(used, highest, top)
    scale = jnp.where(used, total * jnp.exp(safe - top), 0.0)
    coef = scale / jnp.sum(scale, axis=1, keepdims=True)
    coef_rows = jnp.transpose(coef, (0, 1, 3, 2))[..., None]
    mixed = jnp.sum(coef_rows * part.astype(jnp.float32), axis=1)
    return mixed.reshape(groups_here, group_len, local_width).astype(jnp.bfloat16)


def attend_spans(grouped, gathered, counts):
    pair_queries = jnp.repeat(grouped, NBR, axis=0)
    part, highest, total = partial_attend(pair_queries, gathered[:, 0], gathered[:, 1])
    return combine(part, highest, total, counts)


def local_spans(gathered, queries, nbr_count):
    tokens_here = queries.shape[0]
    local_width = queries.shape[1]
    spans_here = nbr_count.shape[0]
    leading = SPAN - 1
    borrowed = passed_along(queries[:leading], "seq", -1)
    grouped = jnp.concatenate([queries[leading:], borrowed], 0).reshape(
        spans_here, SPAN, local_width
    )
    context = attend_spans(grouped, gathered, nbr_count).reshape(tokens_here, local_width)
    carried = passed_along(context[tokens_here - leading :], "seq", 1)
    return jnp.concatenate([carried, context[: tokens_here - leading]], 0)


def shards(hidden, query_weight, out_weight, kv_cache, nbr_shard, nbr_row, nbr_count):
    spans_here = nbr_shard.shape[0]
    peers = lax.axis_size("seq")
    capacity = max(2, 4 * spans_here // peers)
    owners = nbr_shard.reshape(-1)
    wanted = nbr_row.reshape(-1)
    onehot = (owners[:, None] == jnp.arange(peers)[None, :]).astype(jnp.int32)
    slot_rank = jnp.sum((jnp.cumsum(onehot, axis=0) - 1) * onehot, axis=1)
    asked = jnp.zeros((peers, capacity), jnp.int32).at[owners, slot_rank].set(wanted)
    widened = hidden.astype(jnp.float32)
    meansq = jnp.mean(widened * widened, axis=1, keepdims=True)
    normed = (widened * lax.rsqrt(meansq + 1e-05)).astype(jnp.bfloat16)
    queries = jnp.dot(normed, query_weight, preferred_element_type=jnp.float32).astype(jnp.bfloat16)
    picked = kv_cache[lax.all_to_all(asked, "seq", split_axis=0, concat_axis=0, tiled=True)]
    returned = lax.all_to_all(picked, "seq", split_axis=0, concat_axis=0, tiled=True)
    gathered = returned[owners, slot_rank]
    context = local_spans(gathered, queries, nbr_count)
    return lax.psum_scatter(
        jnp.dot(context, out_weight, preferred_element_type=jnp.float32).astype(jnp.bfloat16),
        "tp",
        scatter_dimension=0,
        tiled=True,
    )


def solution(mesh):
    placed = (
        P("seq", None),
        P(None, "tp"),
        P("tp", None),
        P("seq", None, None, "tp"),
        P("seq", None),
        P("seq", None),
        P("seq"),
    )
    return jax.shard_map(
        shards, mesh=mesh, in_specs=placed, out_specs=P(("seq", "tp"), None), check_vma=False
    )
```

profile of v0, /device:TPU:1, one launch (start us, length us, event | category | flops | bytes accessed | tf_op | source)
XLA Modules:
  0.0 407.2 jit_solution(15277064753675283231)
XLA Ops:
  6.5 0.9 copy.39
  7.4 0.1 eq.15
  7.5 0.1 reshape.128
  7.6 0.1 fusion.18
  7.7 0.1 reduce_window_sum.11
  7.8 0.2 select_reduce_fusion.1
  7.9 0.8 copy.41
  8.7 0.1 reshape.149
  8.8 2.0 scatter_fusion
  10.8 0.1 copy.42
  10.9 13.8 %all_to_all.17 = s32[16,1,4]{2,1,0:T(1,128)S(1)} all-to-all(s32[16,1,4]{2,1,0:T(1,128)S(1)} %copy.42), channel_id=1, replica_groups=mesh['seq'=16,'tp'=8] {'seq'}, dimensions={0} | all-to-all | bytes 512 | tf_op jit(solution)/shard_map/all_to_all | solution.py:87
  24.7 0.1 copy.43
  24.8 0.1 copy.44
  24.9 0.1 reshape.135
  25.0 7.4 %gather_fusion = bf16[64,2,128,512]{3,2,1,0:T(8,128)(2,1)} fusion(bf16[8,2,128,512]{3,2,1,0:T(8,128)(2,1)S(1)} %copy-done, s32[1024]{0:T(1024)S(1)} %pad_clamp_fusion), kind=kCustom, calls=%fused_computation | custom fusion | bytes 33554688 | tf_op jit(solution)/shard_map/gather | solution.py:87
  32.4 5.2 %all-to-all-start.1 = ((bf16[16,4,2,128,512]{4,3,2,1,0:T(8,128)(2,1)}), bf16[16,4,2,128,512]{4,3,2,1,0:T(8,128)(2,1)}, u32[]{:S(2)}, u32[]{:S(2)}) async-start(bf16[16,4,2,128,512]{4,3,2,1,0:T(8,128)(2,1)} %bitcast.47), calls=%async_computation.1 | async-start | bytes 33554432 | tf_op jit(solution)/shard_map/all_to_all | solution.py:88
  37.5 0.0 reduce-scatter.2.cloned.1.call-start
  37.6 0.0 copy-start.3
  37.6 5.2 %fusion = f32[1024]{0:T(1024)S(1)} fusion(bf16[1024,4096]{1,0:T(8,128)(2,1)} %param.7), kind=kLoop, calls=%fused_computation.5 | loop fusion | flops 12581888 | bytes 8392704 | tf_op jit(solution)/shard_map/reduce_sum | solution.py:84
  42.8 0.0 copy-start.5
  42.8 7.2 %fusion.12 = bf16[1024,512]{1,0:T(8,128)(2,1)S(1)} fusion(bf16[4096,512]{1,0:T(8,128)(2,1)S(1)} %copy-done.3, bf16[1024,4096]{1,0:T(8,128)(2,1)} %param.7, f32[1024]{0:T(1024)S(1)} %add_rsqrt_fusion), kind=kOutput, calls=%fused_computation.22 | convolution fusion | flops 4308074496 | bytes 13635584 | tf_op jit(solution)/shard_map/dot_general | solution.py:86
  50.0 1.5 collective-permute-start
  51.5 0.1 iota_compare_fusion.1
  51.6 0.2 slice.30
  51.8 230.5 %collective-permute-done = bf16[63,512]{1,0:T(8,128)(2,1)S(1)} collective-permute-done((bf16[63,512]{1,0:T(8,128)(2,1)S(1)}, bf16[63,512]{1,0:T(8,128)(2,1)S(1)}, u32[]{:S(2)}, u32[]{:S(2)}) %collective-permute-start) | collective-permute-done | bytes 64544 | tf_op jit(solution)/shard_map/ppermute | solution.py:14
  282.3 0.1 pad_maximum_fusion
  282.4 1.6 broadcast_in_dim.35
  284.0 2.5 reshape_reshape.4
  286.6 10.9 %gather_fusion.1 = bf16[32,2,128,512]{3,2,1,0:T(8,128)(2,1)} fusion(bf16[16,4,2,128,512]{4,3,2,1,0:T(8,128)(2,1)} %all-to-all-done.1, s32[32]{0:T(128)S(1)} %bitcast.54), kind=kCustom, calls=%fused_computation.1 | custom fusion | bytes 16777472 | tf_op jit(solution)/shard_map/gather | solution.py:89
  297.5 5.9 %fusion.25 = (bf16[32,1,128,512]{3,2,1,0:T(8,128)(2,1)}, bf16[32,1,128,512]{3,2,1,0:T(8,128)(2,1)}) fusion(bf16[32,2,128,512]{3,2,1,0:T(8,128)(2,1)} %gather_fusion.1), kind=kLoop, calls=%fused_computation.49 | loop fusion | bytes 16777216 | tf_op jit(solution)/shard_map/slice | solution.py:56
  303.4 6.4 %copy.45 = bf16[32,1,128,512]{2,3,0,1:T(8,128)(2,1)} copy(bf16[32,1,128,512]{3,2,1,0:T(8,128)(2,1)} %get-tuple-element.8) | data formatting | bytes 8388608 | tf_op jit(solution)/shard_map/slice | solution.py:56
  309.8 3.5 multiply_reduce_fusion.1
  313.3 2.0 copy-done.2
  315.3 2.5 fusion.5
  317.8 0.1 select_reduce_fusion
  317.9 0.1 fusion.23
  318.0 0.1 divide_bitcast_fusion
  318.1 6.4 %copy.48 = bf16[32,1,128,512]{2,3,0,1:T(8,128)(2,1)} copy(bf16[32,1,128,512]{3,2,1,0:T(8,128)(2,1)} %get-tuple-element.7) | data formatting | bytes 8388608 | tf_op jit(solution)/shard_map/slice | solution.py:56
  324.5 5.9 %multiply_reduce_fusion = bf16[16,64,4,128]{3,1,2,0:T(8,128)(2,1)S(1)} fusion(f32[16,2,64,4]{2,3,1,0:T(4,128)S(1)} %divide_bitcast_fusion, bf16[32,128,4,128]{1,3,2,0:T(8,128)(2,1)} %bitcast.48, f32[32,4,64,128]{3,2,1,0:T(8,128)} %copy-done.2, f32[32,4,64]{2,1,0:T(4,128)S(1)} %fusion.5, f32[32,4,64]{2,1,0:T(4,128)S(1)} %get-tuple-element.9), kind=kOutput, calls=%fused_computation.10 | convolution fusion | flops 276299776 | bytes 9535488 | tf_op jit(solution)/shard_map/bhqk,bkhd->bqhd/dot_general | solution.py:32
  330.5 0.0 copy-start.4
  330.5 0.9 copy.50
  331.4 0.2 copy.59
  331.6 1.4 collective-permute-start.1
  333.0 0.1 slice.35
  333.1 1.2 collective-permute-done.1
  334.3 6.7 %convolution_convert_fusion = bf16[1024,4096]{1,0:T(8,128)(2,1)} fusion(bf16[512,4096]{1,0:T(8,128)(2,1)S(1)} %copy-done.4, bf16[961,512]{1,0:T(8,128)(2,1)S(1)} %slice.35, bf16[63,512]{1,0:T(8,128)(2,1)S(1)} %collective-permute-done.1), kind=kOutput, calls=%fused_computation.9 | convolution fusion | flops 4301258752 | bytes 13631488 | tf_op jit(solution)/shard_map/dot_general | solution.py:92
  341.0 0.0 reduce-scatter.2.cloned.1.call-update
  341.0 59.3 %reduce-scatter.2.cloned.1.call-done = bf16[128,4096]{1,0:T(8,128)(2,1)} async-done(((bf16[1024,4096]{1,0:T(8,128)(2,1)}), bf16[128,4096]{1,0:T(8,128)(2,1)}) %reduce-scatter.2.cloned.1.call-update) | async-done | bytes 1048592 | tf_op jit(solution)/shard_map/reduce_scatter | solution.py:91
  (17 shorter events, 0.1 us)
Async XLA Ops:
  6.5 18.5 %copy-start = (bf16[8,2,128,512]{3,2,1,0:T(8,128)(2,1)S(1)}, bf16[8,2,128,512]{3,2,1,0:T(8,128)(2,1)}, u32[]{:S(2)}) copy-start(bf16[8,2,128,512]{3,2,1,0:T(8,128)(2,1)} %param.10) | copy-start | bytes 6291460
  32.4 254.2 %all-to-all-start.1 = ((bf16[16,4,2,128,512]{4,3,2,1,0:T(8,128)(2,1)}), bf16[16,4,2,128,512]{4,3,2,1,0:T(8,128)(2,1)}, u32[]{:S(2)}, u32[]{:S(2)}) async-start(bf16[16,4,2,128,512]{4,3,2,1,0:T(8,128)(2,1)} %bitcast.47), calls=%async_computation.1 | async-start | bytes 33554432 | tf_op jit(solution)/shard_map/all_to_all | solution.py:88
  37.5 362.8 %reduce-scatter.2.cloned.1.call-start = ((), (), s32[]{:S(2)}) async-start(), calls=%async_computation.3 | async-start | bytes 9437184 | tf_op jit(solution)/shard_map/reduce_scatter | solution.py:91
  37.6 5.2 %copy-start.3 = (bf16[4096,512]{1,0:T(8,128)(2,1)S(1)}, bf16[4096,512]{1,0:T(8,128)(2,1)}, u32[]{:S(2)}) copy-start(bf16[4096,512]{1,0:T(8,128)(2,1)} %param.8) | copy-start | bytes 12582916
  42.8 8.7 %copy-start.5 = (s32[16]{0:T(128)S(1)}, s32[16]{0:T(128)}, u32[]{:S(2)}) copy-start(s32[16]{0:T(128)} %param.13) | copy-start | bytes 196
  50.0 232.3 %collective-permute-start = (bf16[63,512]{1,0:T(8,128)(2,1)S(1)}, bf16[63,512]{1,0:T(8,128)(2,1)S(1)}, u32[]{:S(2)}, u32[]{:S(2)}) collective-permute-start(bf16[63,512]{1,0:T(8,128)(2,1)S(1)} %slice.31), channel_id=1, source_target_pairs={{8,0},{16,8},{24,16},{32,24},{40,32},{48,40},{56,48},{64,56},{72,6... | collective-permute-start | bytes 193544 | tf_op jit(solution)/shard_map/ppermute | solution.py:14
  313.3 2.0 copy-start.2
  330.5 3.9 copy-start.4
  331.6 2.7 collective-permute-start.1
  341.0 59.3 %copy-start.1 = (bf16[8,2,128,512]{3,2,1,0:T(8,128)(2,1)S(1)}, bf16[8,2,128,512]{3,2,1,0:T(8,128)(2,1)}, u32[]{:S(2)}) copy-start(bf16[8,2,128,512]{3,2,1,0:T(8,128)(2,1)} %param.10) | copy-start | bytes 6291460
Sparse Core Ops, SparseCore 0:
  341.2 59.1 reduce-scatter.1
where the time goes:
time: 408 us; the launch traced here: 407 us
  waiting for transfers between devices  291 us (71%)
  local copies, waits for them, and re-layouts  48.8 us (12%)
  matrix products  23.3 us (6%)
  blocking collectives  13.8 us (3%)
  between operations  13.6 us (3%)
  other arithmetic  8.52 us (2%)
  starting transfers between devices  8.09 us (2%)
    ppermute x2, waiting for transfers between devices, passed_along(): return lax.ppermute(shard, axis, pairs)  232 us
    reduce_scatter x1, waiting for transfers between devices, shards(): lax.psum_scatter(jnp.dot(context, out_weight, preferred_element_type=jnp....  59.3 us
    all_to_all x1, blocking collectives, shards(): lax.all_to_all(asked, 'seq', split_axis=0, concat_axis=0, tiled=True)  13.8 us
    slice x2, local copies, waits for them, and re-layouts, attend_spans(): gathered[:, 1]  12.3 us
    gather x1, local copies, waits for them, and re-layouts, shards(): gathered = returned[owners, slot_rank]  10.9 us
  transfers between devices with their start and end apart: 4, of which 3 were waited for; matrix products, arithmetic and copies ran while one was open for 4% of the time, Pallas kernels for 0%

commit v1 on v0

v1 whole, which is shorter than its diff:
```python
import functools

import jax
import jax.numpy as jnp
from jax import lax
from jax.experimental import pallas as pl
from jax.experimental.pallas import tpu as pltpu
from jax.sharding import PartitionSpec as P

F32 = jnp.float32
BF16 = jnp.bfloat16
HEAD = 128
SPAN = 64
SIDE = 4
CAP = 4
HEADS = 4
GROUPS = 16
WIDTH = HEADS * HEAD
OFFSET = (0, -1, 1, 2)
FAR = -1e30
SCORE = 1.4426950408889634 * HEAD**-0.5


def kernel(
    hidden,
    wq,
    wo,
    kv,
    table,
    out,
    hid_v,
    wq_v,
    w2,
    kv_0,
    kv_1,
    kv_2,
    kv_3,
    q_0,
    q_1,
    q_2,
    q_3,
    parts,
    lses,
    tab_v,
    tab_s,
    borrowed,
    sent,
    stats,
    opp,
    opp_stats,
    back,
    back_stats,
    ctx,
    carried,
    far_part,
    far_got,
    near_part,
    near_got,
    own_part,
    swap,
    hid_sem,
    load_sem,
    tab_sem,
    kv_sem,
    q_sem,
    t_sem,
    b_sem,
    w_sem,
    r_sem,
    x_sem,
    z_sem,
    s_sem,
):
    kvbuf = (kv_0, kv_1, kv_2, kv_3)
    qbuf = (q_0, q_1, q_2, q_3)
    seq = lax.axis_index("seq")
    tp = lax.axis_index("tp")
    core = tp % 2
    z = tp // 2
    row, col = seq // SIDE, seq % SIDE
    a = row + core * (col - row)
    b = col + core * (row - col)
    a_step, b_step = SIDE - 3 * core, 1 + 3 * core

    def along_a(by):
        return (lax.rem(a + by + SIDE, SIDE) * a_step + b * b_step, tp)

    def along_b(by):
        return (a * a_step + lax.rem(b + by + SIDE, SIDE) * b_step, tp)

    def along_z(by):
        return (seq, lax.rem(z + by + SIDE, SIDE) * 2 + core)

    sibling = (seq, z * 2 + 1 - core)
    next_block = (lax.rem(seq + 1, 16), tp)
    last_block = (lax.rem(seq + 15, 16), tp)

    def remote(src, dst, sems, at, device):
        return pltpu.make_async_remote_copy(
            src_ref=src,
            dst_ref=dst,
            send_sem=sems.at[0, at],
            recv_sem=sems.at[1, at],
            device_id=device,
            device_id_type=pl.DeviceIdType.MESH,
        )

    started = []

    def send(copy):
        copy.start()
        started.append(copy)

    loads = [pltpu.make_async_copy(wq, wq_v, load_sem.at[0])]
    loads[0].start()
    hid_loads = [
        pltpu.make_async_copy(hidden.at[pl.ds(256 * c, 256), :], hid_v.at[c], hid_sem.at[c])
        for c in range(4)
    ]
    for copy in hid_loads:
        copy.start()
    kv_load = pltpu.make_async_copy(kv, kvbuf[0], load_sem.at[1])
    kv_load.start()
    tab_load = pltpu.make_async_copy(table, tab_s.at[0], tab_sem.at[0])
    tab_load.start()
    w_load = pltpu.make_async_copy(
        wo.at[:, pl.ds(pl.multiple_of(core * 2048, 2048), 2048)], w2.at[core], load_sem.at[2]
    )
    w_load.start()

    barrier = pltpu.get_barrier_semaphore()
    friends = (
        along_a(1), along_a(-1), along_b(1), along_b(-1), along_z(1), along_z(-1),
        sibling, next_block, last_block,
    )
    for device in friends:
        pl.semaphore_signal(barrier, inc=1, device_id=device, device_id_type=pl.DeviceIdType.MESH)
    pl.semaphore_wait(barrier, len(friends))

    low, high = pl.ds(0, 4), pl.ds(4, 4)
    kv_copies = [
        remote(kv.at[low], kvbuf[1].at[low], kv_sem, 0, along_a(1)),
        remote(kv.at[high], kvbuf[2].at[high], kv_sem, 1, along_a(-1)),
        remote(kv.at[high], kvbuf[1].at[high], kv_sem, 2, along_a(1)),
        remote(kv.at[low], kvbuf[2].at[low], kv_sem, 3, along_a(-1)),
        remote(kvbuf[1].at[low], kvbuf[3].at[low], kv_sem, 4, along_a(1)),
        remote(kvbuf[2].at[high], kvbuf[3].at[high], kv_sem, 5, along_a(-1)),
    ]
    for copy in kv_copies[:4]:
        send(copy)
    tab_copies = [
        remote(table, tab_v.at[0], t_sem, 0, along_b(1)),
        remote(table, tab_v.at[1], t_sem, 1, along_b(-1)),
        remote(tab_v.at[0], tab_v.at[2], t_sem, 2, along_b(1)),
    ]
    for copy in tab_copies[:2]:
        send(copy)
    w_copy = remote(
        wo.at[:, pl.ds(pl.multiple_of((1 - core) * 2048, 2048), 2048)], w2.at[core], w_sem, 0, sibling
    )

    lo_g, hi_g = pl.ds(0, 8), pl.ds(8, 8)
    q_copies = [
        remote(qbuf[0].at[lo_g], qbuf[1].at[lo_g], q_sem, 0, along_b(1)),
        remote(qbuf[0].at[hi_g], qbuf[2].at[hi_g], q_sem, 1, along_b(-1)),
        remote(qbuf[0].at[hi_g], qbuf[1].at[hi_g], q_sem, 2, along_b(1)),
        remote(qbuf[0].at[lo_g], qbuf[2].at[lo_g], q_sem, 3, along_b(-1)),
        remote(qbuf[1].at[lo_g], qbuf[3].at[lo_g], q_sem, 4, along_b(1)),
        remote(qbuf[2].at[hi_g], qbuf[3].at[hi_g], q_sem, 5, along_b(-1)),
    ]
    lend = remote(borrowed.at[0], borrowed.at[1], b_sem, 0, last_block)
    loads[0].wait()
    tail = jnp.zeros((1, WIDTH), F32)
    first_row = lax.broadcasted_iota(jnp.int32, (256, WIDTH), 0) == 0
    for c in range(4):
        hid_loads[c].wait()
        square = jnp.zeros((256, HEAD), F32)
        for j in range(32):
            piece = hid_v[c, :, j * HEAD : (j + 1) * HEAD].astype(F32)
            square = square + piece * piece
        scale = lax.rsqrt(jnp.sum(square, axis=1, keepdims=True) * (1.0 / 4096) + 1e-05)
        cols = [
            jnp.dot(hid_v[c], wq_v[:, n * 256 : (n + 1) * 256], preferred_element_type=F32) * scale
            for n in range(2)
        ]
        queries = jnp.concatenate(cols, axis=1)
        moved = jnp.where(first_row, tail, pltpu.roll(queries, 1, 0))
        tail = queries[255:256]
        moved = moved.astype(BF16).reshape(4, SPAN, WIDTH)
        if c == 0:
            borrowed[0] = moved[0]
            send(lend)
            qbuf[0][0:3] = moved[1:4]
        else:
            qbuf[0][4 * c - 1 : 4 * c + 3] = moved
        if c == 2:
            send(q_copies[0])
            send(q_copies[3])
    lend.wait_recv()
    span_row = lax.broadcasted_iota(jnp.int32, (SPAN, WIDTH), 0)
    qbuf[0][15] = jnp.where(span_row == 0, tail, borrowed[1].astype(F32)).astype(BF16)
    send(q_copies[1])
    send(q_copies[2])
    send(w_copy)

    tab_copies[0].wait_recv()
    send(tab_copies[2])
    tab_copies[1].wait_recv()
    tab_copies[2].wait_recv()
    tab_loads = [
        pltpu.make_async_copy(tab_v.at[d], tab_s.at[d + 1], tab_sem.at[d + 1]) for d in range(3)
    ]
    for copy in tab_loads:
        copy.start()
    for copy in [tab_load, *tab_loads]:
        copy.wait()
    kv_load.wait()

    lane = lax.broadcasted_iota(jnp.int32, (SPAN, HEAD), 1)

    def slots(d, i):
        base = lax.rem(a + OFFSET[i] + SIDE, SIDE) * CAP

        def one(k, carry):
            at = base + k
            group = tab_s[d, b, at]
            cached = tab_s[d, b, 16 + at]
            lse = jnp.zeros((SPAN, HEAD), F32)
            for h in range(HEADS):
                cut = slice(h * HEAD, (h + 1) * HEAD)
                query = qbuf[d][group, :, cut]
                keys = kvbuf[i][cached, 0, :, cut]
                values = kvbuf[i][cached, 1, :, cut]
                scores = lax.dot_general(
                    query, keys, (((1,), (1,)), ((), ())), preferred_element_type=F32
                )
                scores = scores * SCORE
                highest = jnp.max(scores, axis=1, keepdims=True)
                expon = jnp.exp2(scores - highest)
                total = jnp.sum(expon, axis=1, keepdims=True)
                part = jnp.dot(expon.astype(BF16), values, preferred_element_type=F32)
                parts[d, at, :, cut] = (part / total).astype(BF16)
                lse = jnp.where(lane == h, highest + jnp.log2(total), lse)
            lses[d, at] = lse
            return carry

        lax.fori_loop(0, CAP, one, 0)

    def merged(sources):
        top = functools.reduce(jnp.maximum, [lse for lse, _ in sources])
        shares = [jnp.exp2(lse - top) for lse, _ in sources]
        whole = functools.reduce(jnp.add, shares)
        inverse = 1.0 / whole
        coefs = [share * inverse for share in shares]
        heads = []
        for h in range(HEADS):
            cut = slice(h * HEAD, (h + 1) * HEAD)
            heads.append(
                functools.reduce(
                    jnp.add,
                    [
                        coef[:, h : h + 1] * part[:, cut].astype(F32)
                        for coef, (_, part) in zip(coefs, sources)
                    ],
                )
            )
        return jnp.concatenate(heads, axis=1), top + jnp.log2(whole)

    def from_slots(d, g):
        found = []
        for n in range(2):
            at = tab_s[d, b, 32 + 2 * g + n]
            used = tab_s[d, b, 64 + 2 * g + n]
            lse = jnp.where(jnp.full((SPAN, HEAD), used, jnp.int32) > 0, lses[d, at], FAR)
            found.append((lse, parts[d, at]))
        return found

    def stats_of(held, g):
        return pltpu.roll(held, lax.rem(HEAD - HEADS * g, HEAD), 1)

    def contribute(d, first, last, extra, held):
        def one(g, held):
            sources = from_slots(d, g)
            if extra is not None:
                sources.append((stats_of(opp_stats[extra], g), opp[extra, g - first]))
            mixed, lse = merged(sources)
            sent[d - 1, g] = mixed.astype(BF16)
            return jnp.where(lane // HEADS == g, pltpu.roll(lse, HEADS * g, 1), held)

        return lax.fori_loop(first, last, one, held)

    kv_copies[0].wait_recv()
    send(kv_copies[4])
    kv_copies[1].wait_recv()
    send(kv_copies[5])
    q_copies[0].wait_recv()
    send(q_copies[4])
    q_copies[1].wait_recv()
    send(q_copies[5])
    slots(0, 0)
    q_copies[2].wait_recv()
    q_copies[3].wait_recv()
    slots(1, 0)
    slots(2, 0)
    kv_copies[2].wait_recv()
    kv_copies[3].wait_recv()
    for d in range(3):
        slots(d, 1)
        slots(d, 2)
    q_copies[4].wait_recv()
    q_copies[5].wait_recv()
    for i in range(3):
        slots(3, i)
    kv_copies[4].wait_recv()
    kv_copies[5].wait_recv()

    none = jnp.zeros((SPAN, HEAD), F32)
    opp_copies = [
        remote(sent.at[2, lo_g], opp.at[0], r_sem, 0, along_b(1)),
        remote(stats.at[2], opp_stats.at[0], r_sem, 1, along_b(1)),
        remote(sent.at[2, hi_g], opp.at[1], r_sem, 2, along_b(-1)),
        remote(stats.at[2], opp_stats.at[1], r_sem, 3, along_b(-1)),
    ]
    back_copies = [
        remote(sent.at[1, hi_g], back.at[0, hi_g], r_sem, 4, along_b(1)),
        remote(sent.at[1, lo_g], back.at[0, lo_g], r_sem, 5, along_b(1)),
        remote(stats.at[1], back_stats.at[0], r_sem, 6, along_b(1)),
        remote(sent.at[0, lo_g], back.at[1, lo_g], r_sem, 7, along_b(-1)),
        remote(sent.at[0, hi_g], back.at[1, hi_g], r_sem, 8, along_b(-1)),
        remote(stats.at[0], back_stats.at[1], r_sem, 9, along_b(-1)),
    ]
    slots(3, 3)
    stats[2] = contribute(3, 0, GROUPS, None, none)
    for copy in opp_copies:
        send(copy)
    slots(2, 3)
    held_next = contribute(2, 8, GROUPS, None, none)
    send(back_copies[0])
    slots(1, 3)
    held_last = contribute(1, 0, 8, None, none)
    send(back_copies[3])
    slots(0, 3)
    opp_copies[0].wait_recv()
    opp_copies[1].wait_recv()
    stats[1] = contribute(2, 0, 8, 0, held_next)
    send(back_copies[1])
    send(back_copies[2])
    opp_copies[2].wait_recv()
    opp_copies[3].wait_recv()
    stats[0] = contribute(1, 8, GROUPS, 1, held_last)
    send(back_copies[4])
    send(back_copies[5])
    for copy in back_copies:
        copy.wait_recv()

    carry_copy = remote(carried.at[0], carried.at[1], b_sem, 1, next_block)

    def finish(g):
        sources = from_slots(0, g)
        sources.append((stats_of(back_stats[0], g), back[0, g]))
        sources.append((stats_of(back_stats[1], g), back[1, g]))
        return merged(sources)[0]

    mixed = finish(GROUPS - 1)
    carried[0] = pltpu.roll(mixed, SPAN - 1, 0).astype(BF16)
    send(carry_copy)

    def one_span(step, head_row):
        g = GROUPS - 2 - step
        mixed = finish(g)
        moved = jnp.where(span_row == SPAN - 1, head_row, pltpu.roll(mixed, SPAN - 1, 0))
        ctx[core, g + 1] = moved.astype(BF16)
        return mixed[0:1]

    head_row = lax.fori_loop(0, GROUPS - 1, one_span, mixed[0:1])
    carry_copy.wait_recv()
    arrived = jnp.where(jnp.full((SPAN, WIDTH), seq, jnp.int32) > 0, carried[1].astype(F32), 0.0)
    ctx[core, 0] = jnp.where(span_row == SPAN - 1, head_row, arrived).astype(BF16)

    ctx_copy = remote(ctx.at[core], ctx.at[core], x_sem, 0, sibling)
    send(ctx_copy)
    w_load.wait()
    w_copy.wait_recv()
    ctx_copy.wait_recv()

    def project(by, half, write):
        start = lax.rem(z + by + SIDE, SIDE) * 4
        left = ctx[0, pl.ds(start, 4)].reshape(256, WIDTH)
        right = ctx[1, pl.ds(start, 4)].reshape(256, WIDTH)

        def one(n, carry):
            at = pl.ds(pl.multiple_of(half * 1024 + n * 256, 256), 256)
            total = jnp.dot(left, w2[0, :, at], preferred_element_type=F32)
            total = total + jnp.dot(right, w2[1, :, at], preferred_element_type=F32)
            write(pl.ds(pl.multiple_of(n * 256, 256), 256), total)
            return carry

        lax.fori_loop(0, 4, one, 0)

    far_copies = [
        remote(far_part.at[0], far_got.at[0], z_sem, 0, along_z(1)),
        remote(far_part.at[1], far_got.at[1], z_sem, 1, along_z(-1)),
    ]
    near_copies = [
        [remote(near_part.at[0, h], near_got.at[0, h], z_sem, 2 + h, along_z(1)) for h in range(2)],
        [remote(near_part.at[1, h], near_got.at[1, h], z_sem, 4 + h, along_z(-1)) for h in range(2)],
    ]

    for half in range(2):

        def write_far(at, total, half=half):
            far_part[half, :, at] = total.astype(BF16)

        project(2, half, write_far)
        send(far_copies[half])

    def near(way, half, got):
        def write_near(at, total):
            if got is not None:
                total = total + far_got[got, :, at].astype(F32)
            near_part[way, half, :, at] = total.astype(BF16)

        project(1 - 2 * way, half, write_near)
        send(near_copies[way][half])

    near(0, 1, None)
    near(1, 0, None)
    far_copies[0].wait_recv()
    near(0, 0, 0)
    far_copies[1].wait_recv()
    near(1, 1, 1)

    mine = pl.ds(pl.multiple_of(core * 128, 128), 128)
    theirs = pl.ds(pl.multiple_of((1 - core) * 128, 128), 128)
    swap_copies = [
        remote(own_part.at[half, theirs], swap.at[half], s_sem, half, sibling) for half in range(2)
    ]
    for half in (1, 0):
        near_copies[0][half].wait_recv()
        near_copies[1][half].wait_recv()

        def write_own(at, total, half=half):
            total = total + near_got[0, half, :, at].astype(F32)
            total = total + near_got[1, half, :, at].astype(F32)
            own_part[half, :, at] = total.astype(BF16)

        project(0, half, write_own)
        send(swap_copies[half])
        out[:, pl.ds(pl.multiple_of(core * 2048 + half * 1024, 1024), 1024)] = own_part[half, mine]
    for half in (1, 0):
        swap_copies[half].wait_recv()
        out[:, pl.ds(pl.multiple_of((1 - core) * 2048 + half * 1024, 1024), 1024)] = swap[half]
    for copy in started:
        copy.wait_send()


def tables(nbr_shard, nbr_row, nbr_count):
    core = lax.axis_index("tp") % 2
    owners = nbr_shard.reshape(-1)
    wanted = nbr_row.reshape(-1)
    pairs = owners.shape[0]
    at = jnp.arange(pairs)
    before = (owners[:, None] == owners[None, :]) & (at[None, :] < at[:, None])
    rank = jnp.sum(before.astype(jnp.int32), axis=1)
    used = (at % 2) < jnp.maximum(nbr_count, 1)[at // 2]
    owner_a = jnp.where(core == 0, owners // SIDE, owners % SIDE)
    owner_b = jnp.where(core == 0, owners % SIDE, owners // SIDE)
    slot = owner_a * CAP + rank
    ring = jnp.arange(8)[:, None]
    here = owner_b[None, :] == ring
    match = here[:, None, :] & (slot[None, None, :] == jnp.arange(16)[None, :, None])
    group_at = jnp.sum(jnp.where(match, (at // 2)[None, None, :], 0), axis=2)
    row_at = jnp.sum(jnp.where(match, wanted[None, None, :], 0), axis=2)
    slot_at = jnp.where(here, slot[None, :], 0)
    used_at = (here & used[None, :]).astype(jnp.int32)
    filler = jnp.zeros((8, 32), jnp.int32)
    return jnp.concatenate([group_at, row_at, slot_at, used_at, filler], axis=1).astype(jnp.int32)


def shards(hidden, query_weight, out_weight, kv_cache, nbr_shard, nbr_row, nbr_count):
    table = tables(nbr_shard, nbr_row, nbr_count)
    dma = pltpu.SemaphoreType.DMA
    hbm = pl.BlockSpec(memory_space=pl.ANY)
    return pl.pallas_call(
        kernel,
        out_shape=jax.ShapeDtypeStruct((128, 4096), BF16),
        in_specs=[hbm] * 5,
        out_specs=pl.BlockSpec(memory_space=pltpu.VMEM),
        scratch_shapes=[
            pltpu.VMEM((4, 256, 4096), BF16),
            pltpu.VMEM((4096, WIDTH), BF16),
            pltpu.VMEM((2, WIDTH, 2048), BF16),
            *[pltpu.VMEM((8, 2, 128, WIDTH), BF16)] * 4,
            *[pltpu.VMEM((GROUPS, SPAN, WIDTH), BF16)] * 4,
            pltpu.VMEM((4, 16, SPAN, WIDTH), BF16),
            pltpu.VMEM((4, 16, SPAN, HEAD), F32),
            pltpu.VMEM((3, 8, 128), jnp.int32),
            pltpu.SMEM((4, 8, 128), jnp.int32),
            pltpu.VMEM((2, SPAN, WIDTH), BF16),
            pltpu.VMEM((3, GROUPS, SPAN, WIDTH), BF16),
            pltpu.VMEM((3, SPAN, HEAD), F32),
            pltpu.VMEM((2, 8, SPAN, WIDTH), BF16),
            pltpu.VMEM((2, SPAN, HEAD), F32),
            pltpu.VMEM((2, GROUPS, SPAN, WIDTH), BF16),
            pltpu.VMEM((2, SPAN, HEAD), F32),
            pltpu.VMEM((2, GROUPS, SPAN, WIDTH), BF16),
            pltpu.VMEM((2, SPAN, WIDTH), BF16),
            pltpu.VMEM((2, 256, 1024), BF16),
            pltpu.VMEM((2, 256, 1024), BF16),
            pltpu.VMEM((2, 2, 256, 1024), BF16),
            pltpu.VMEM((2, 2, 256, 1024), BF16),
            pltpu.VMEM((2, 256, 1024), BF16),
            pltpu.VMEM((2, 128, 1024), BF16),
            dma((4,)),
            dma((3,)),
            dma((4,)),
            dma((2, 6)),
            dma((2, 6)),
            dma((2, 3)),
            dma((2, 2)),
            dma((2, 1)),
            dma((2, 10)),
            dma((2, 1)),
            dma((2, 6)),
            dma((2, 2)),
        ],
        compiler_params=pltpu.CompilerParams(
            collective_id=0, has_side_effects=True, vmem_limit_bytes=62 * 1024 * 1024
        ),
        cost_estimate=pl.CostEstimate(flops=9_000_000_000, bytes_accessed=20_000_000, transcendentals=2_000_000),
    )(hidden, query_weight, out_weight, kv_cache, table)


def solution(mesh):
    placed = (
        P("seq", None),
        P(None, "tp"),
        P("tp", None),
        P("seq", None, None, "tp"),
        P("seq", None),
        P("seq", None),
        P("seq"),
    )
    return jax.shard_map(
        shards, mesh=mesh, in_specs=placed, out_specs=P(("seq", "tp"), None), check_vma=False
    )
```

time: 408 us -> 200 us (0.49)
  waiting for transfers between devices: 291 us -> 0 us
  Pallas kernels: 0 us -> 193 us
  local copies, waits for them, and re-layouts: 48.8 us -> 5.35 us
  matrix products: 23.3 us -> 0 us
  blocking collectives: 13.8 us -> 0 us
  between operations: 13.6 us -> 0.08 us
  starting transfers between devices: 8.09 us -> 0 us
  other arithmetic: 8.52 us -> 1.27 us
    ppermute x2 -> x0, waiting for transfers between devices: 232 us -> none  [passed_along(): return lax.ppermute(shard, axis, pairs)]
    pallas_call x0 -> x1, Pallas kernels: none -> 193 us  [shards(): pl.pallas_call(kernel, out_shape=jax.ShapeDtypeStruct((128, 4096), BF16),...]
    reduce_scatter x1 -> x0, waiting for transfers between devices: 59.3 us -> none  [shards(): lax.psum_scatter(jnp.dot(context, out_weight, preferred_element_type=jnp....]
    dot_general x4 -> x0, matrix products: 23.3 us -> none  [the longest x1 7.17 us: shards(): jnp.dot(normed, query_weight, preferred_element_type=jnp.float32)]
    slice x7 -> x0, local copies, waits for them, and re-layouts: 19 us -> none  [the longest x2 12.3 us: attend_spans(): gathered[:, 1]]
    gather x2 -> x1, local copies, waits for them, and re-layouts: 18.3 us -> 0.7 us  [tables(): used = at % 2 < jnp.maximum(nbr_count, 1)[at // 2]]
    all_to_all x1 -> x0, blocking collectives: 13.8 us -> none  [shards(): lax.all_to_all(asked, 'seq', split_axis=0, concat_axis=0, tiled=True)]
    reduce_sum x4 -> x2, other arithmetic: 7.98 us -> 0.53 us  [the longest x1 0.36 us: tables(): row_at = jnp.sum(jnp.where(match, wanted[None, None, :], 0), axis=2)]
  transfers between devices with their start and end apart: 4 -> 0, of which waited for: 3 -> 0; matrix products, arithmetic and copies ran while one was open for 4% -> 0% of each run, Pallas kernels for 0% -> 0%
where the time goes in v1:
time: 200 us
  Pallas kernels  193 us (96%)
  local copies, waits for them, and re-layouts  5.35 us (3%)
    pallas_call x1, Pallas kernels, shards(): pl.pallas_call(kernel, out_shape=jax.ShapeDtypeStruct((128, 4096), BF16),...  193 us

profile of v1, /device:TPU:1, one launch (start us, length us, event | category | flops | bytes accessed | tf_op | source)
XLA Modules:
  0.0 199.7 jit_solution(1674602703705189438)
XLA Ops:
  0.0 0.7 broadcast_maximum_fusion
  0.7 0.7 gather_fusion
  1.4 0.8 copy.12
  2.2 0.1 reshape.237
  2.3 0.2 convert_reduce_fusion
  2.5 0.8 copy.13
  3.3 0.1 broadcast_in_dim.46
  3.4 0.4 fusion.1
  3.7 0.7 concatenate.3.table
  4.4 193.0 %shard_map.73 = bf16[128,4096]{1,0:T(8,128)(2,1)} custom-call(bf16[1024,4096]{1,0:T(8,128)(2,1)} %hidden.1, bf16[4096,512]{1,0:T(8,128)(2,1)} %wq.1, bf16[512,4096]{1,0:T(8,128)(2,1)} %wo.1, bf16[8,2,128,512]{3,2,1,0:T(8,128)(2,1)} %kv.1, s32[8,128]{1,0:T(8,128)} %concatenate.3.table), custom_call_target="tpu_custom_call" | custom-call | flops 8999999488 | bytes 20000000 | tf_op jit(solution)/shard_map/pallas_call | solution.py:484
  197.5 2.3 %copy.15 = bf16[128,4096]{1,0:T(8,128)(2,1)} copy(bf16[128,4096]{1,0:T(8,128)(2,1)} %shard_map.73) | data formatting | bytes 2097152
  (10 shorter events, 0.1 us)

commit v2 on v0

v2 whole, which is shorter than its diff:
```python
import functools

import jax
import jax.numpy as jnp
from jax import lax
from jax.experimental import pallas as pl
from jax.experimental.pallas import tpu as pltpu
from jax.sharding import PartitionSpec as P

F32 = jnp.float32
BF16 = jnp.bfloat16
HEAD = 128
SPAN = 64
SIDE = 4
CAP = 4
HEADS = 4
GROUPS = 16
WIDTH = HEADS * HEAD
OFFSET = (0, -1, 1, 2)
FAR = -1e30
SCORE = 1.4426950408889634 * HEAD**-0.5


def slot_table(core, shard_of, row_of, count_of):
    ring = lax.broadcasted_iota(jnp.int32, (8, 128), 0)
    lane = lax.broadcasted_iota(jnp.int32, (8, 128), 1)
    table = jnp.zeros((8, 128), jnp.int32)
    pairs = 2 * GROUPS
    owners = [shard_of[e % 2, e // 2] for e in range(pairs)]
    for e, owner in enumerate(owners):
        rank = jnp.int32(0)
        for other in owners[:e]:
            rank = rank + jnp.where(other == owner, 1, 0)
        down, across = owner // SIDE, owner % SIDE
        owner_a = down + core * (across - down)
        owner_b = across + core * (down - across)
        slot = owner_a * CAP + jnp.minimum(rank, CAP - 1)
        fits = jnp.where(rank < CAP, 0, 96)
        entry = jnp.where(lane == slot + fits, e // 2, 0)
        entry = entry + jnp.where(lane == 16 + slot + fits, row_of[e % 2, e // 2], 0)
        entry = entry + jnp.where(lane == 32 + e, slot, 0)
        if e % 2 == 0:
            used = jnp.int32(1)
        else:
            used = jnp.where(count_of[e // 2] > 1, 1, 0)
        entry = entry + jnp.where(lane == 64 + e, used, 0)
        table = table + jnp.where(ring == owner_b, entry, 0)
    return table


def kernel(
    hidden, wq, wo, kv, shard_of, row_of, count_of, out,
    hid_v, wq_v, w_all, kvs, qs, parts, lses, table, tab_v, tab_s, borrowed, sent, stats, opp, opp_stats,
    back, back_stats, ctx, carried, total, keep, give, got, ship, landed,
    hid_sem, load_sem, tab_sem, kv_sem, q_sem, t_sem, b_sem, c_sem, w_sem, r_sem, x_sem, g_sem, s_sem,
):
    seq = lax.axis_index("seq")
    tp = lax.axis_index("tp")
    core = tp % 2
    z = tp // 2
    row, col = seq // SIDE, seq % SIDE
    a = row + core * (col - row)
    b = col + core * (row - col)
    a_step, b_step = SIDE - 3 * core, 1 + 3 * core

    def along_a(by):
        return (lax.rem(a + by + SIDE, SIDE) * a_step + b * b_step, tp)

    def along_b(by):
        return (a * a_step + lax.rem(b + by + SIDE, SIDE) * b_step, tp)

    def along_z(by):
        return (seq, lax.rem(z + by + SIDE, SIDE) * 2 + core)

    sibling = (seq, z * 2 + 1 - core)
    next_block = (lax.rem(seq + 1, 16), tp)
    last_block = (lax.rem(seq + 15, 16), tp)

    def remote(src, dst, sems, at, device):
        return pltpu.make_async_remote_copy(
            src_ref=src,
            dst_ref=dst,
            send_sem=sems.at[(0, *at)],
            recv_sem=sems.at[(1, *at)],
            device_id=device,
            device_id_type=pl.DeviceIdType.MESH,
        )

    started = []

    def send(copy):
        copy.start()
        started.append(copy)

    def arrive(*copies):
        for copy in copies:
            copy.wait_recv()

    wq_load = pltpu.make_async_copy(wq, wq_v, load_sem.at[0])
    wq_load.start()
    hid_loads = [
        pltpu.make_async_copy(hidden.at[pl.ds(256 * c, 256), :], hid_v.at[c], hid_sem.at[c])
        for c in range(4)
    ]
    for copy in hid_loads:
        copy.start()
    lanes = [pl.ds(h * HEAD, HEAD) for h in range(HEADS)]
    kv_loads = [
        pltpu.make_async_copy(kv.at[:, :, :, lanes[h]], kvs[0][h], load_sem.at[1 + h])
        for h in range(HEADS)
    ]
    for copy in kv_loads:
        copy.start()

    def columns(of):
        return pl.ds(pl.multiple_of(of * 1024, 1024), 1024)

    w_load = pltpu.make_async_copy(wo.at[:, columns(z)], w_all.at[z], load_sem.at[5])
    w_load.start()

    barrier = pltpu.get_barrier_semaphore()
    friends = (
        along_a(1), along_a(-1), along_b(1), along_b(-1), along_z(1), along_z(-1), along_z(2),
        sibling, next_block, last_block,
    )
    for device in friends:
        pl.semaphore_signal(barrier, inc=1, device_id=device, device_id_type=pl.DeviceIdType.MESH)
    pl.semaphore_wait(barrier, len(friends))

    low, high = pl.ds(0, 4), pl.ds(4, 4)
    kv_copies = [
        [
            remote(kv.at[low, :, :, lanes[h]], kvs[1][h].at[low], kv_sem, (h, 0), along_a(1)),
            remote(kv.at[high, :, :, lanes[h]], kvs[2][h].at[high], kv_sem, (h, 1), along_a(-1)),
            remote(kv.at[high, :, :, lanes[h]], kvs[1][h].at[high], kv_sem, (h, 2), along_a(1)),
            remote(kv.at[low, :, :, lanes[h]], kvs[2][h].at[low], kv_sem, (h, 3), along_a(-1)),
            remote(kvs[1][h].at[low], kvs[3][h].at[low], kv_sem, (h, 4), along_a(1)),
            remote(kvs[2][h].at[high], kvs[3][h].at[high], kv_sem, (h, 5), along_a(-1)),
        ]
        for h in range(HEADS)
    ]
    tab_copies = [
        remote(table, tab_v.at[0], t_sem, (0,), along_b(1)),
        remote(table, tab_v.at[1], t_sem, (1,), along_b(-1)),
        remote(tab_v.at[0], tab_v.at[2], t_sem, (2,), along_b(1)),
    ]
    w_copies = [
        remote(wo.at[:, columns(lax.rem(z + by + SIDE, SIDE))], w_all.at[z], w_sem, (j,), along_z(by))
        for j, by in enumerate((1, -1, 2))
    ]
    for h in range(2):
        for copy in kv_copies[h][:4]:
            send(copy)
    table[...] = slot_table(core, shard_of, row_of, count_of)
    for copy in tab_copies[:2]:
        send(copy)
    tab_load = pltpu.make_async_copy(table, tab_s.at[0], tab_sem.at[0])
    tab_load.start()
    for copy in w_copies:
        send(copy)

    lo_g, hi_g = pl.ds(0, 8), pl.ds(8, 8)
    q_copies = [
        [
            remote(qs[0][h].at[lo_g], qs[1][h].at[lo_g], q_sem, (h, 0), along_b(1)),
            remote(qs[0][h].at[hi_g], qs[2][h].at[hi_g], q_sem, (h, 1), along_b(-1)),
            remote(qs[0][h].at[hi_g], qs[1][h].at[hi_g], q_sem, (h, 2), along_b(1)),
            remote(qs[0][h].at[lo_g], qs[2][h].at[lo_g], q_sem, (h, 3), along_b(-1)),
            remote(qs[1][h].at[lo_g], qs[3][h].at[lo_g], q_sem, (h, 4), along_b(1)),
            remote(qs[2][h].at[hi_g], qs[3][h].at[hi_g], q_sem, (h, 5), along_b(-1)),
        ]
        for h in range(HEADS)
    ]
    lend = remote(borrowed.at[0], borrowed.at[1], b_sem, (), last_block)
    wq_load.wait()
    tail = jnp.zeros((1, WIDTH), F32)
    first_row = lax.broadcasted_iota(jnp.int32, (256, WIDTH), 0) == 0
    for c in range(4):
        hid_loads[c].wait()
        square = jnp.zeros((256, HEAD), F32)
        for j in range(32):
            piece = hid_v[c, :, j * HEAD : (j + 1) * HEAD].astype(F32)
            square = square + piece * piece
        scale = lax.rsqrt(jnp.sum(square, axis=1, keepdims=True) * (1.0 / 4096) + 1e-05)
        cols = [
            jnp.dot(hid_v[c], wq_v[:, n * 256 : (n + 1) * 256], preferred_element_type=F32) * scale
            for n in range(2)
        ]
        queries = jnp.concatenate(cols, axis=1)
        moved = jnp.where(first_row, tail, pltpu.roll(queries, 1, 0))
        tail = queries[255:256]
        moved = moved.astype(BF16).reshape(4, SPAN, WIDTH)
        if c == 0:
            borrowed[0] = moved[0]
            send(lend)
        for h in range(HEADS):
            cut = slice(h * HEAD, (h + 1) * HEAD)
            if c == 0:
                qs[0][h][0:3] = moved[1:4, :, cut]
            else:
                qs[0][h][4 * c - 1 : 4 * c + 3] = moved[:, :, cut]
        if c == 2:
            send(q_copies[0][0])
            send(q_copies[0][3])
    arrive(lend)
    span_row = lax.broadcasted_iota(jnp.int32, (SPAN, HEAD), 0)
    for h in range(HEADS):
        cut = slice(h * HEAD, (h + 1) * HEAD)
        last = jnp.where(span_row == 0, tail[:, cut], borrowed[1, :, cut].astype(F32))
        qs[0][h][15] = last.astype(BF16)
    send(q_copies[0][1])
    send(q_copies[0][2])
    for copy in q_copies[1][:4]:
        send(copy)

    arrive(tab_copies[0])
    send(tab_copies[2])
    arrive(tab_copies[1], tab_copies[2])
    tab_loads = [
        pltpu.make_async_copy(tab_v.at[d], tab_s.at[d + 1], tab_sem.at[d + 1]) for d in range(3)
    ]
    for copy in tab_loads:
        copy.start()
    for copy in [tab_load, *tab_loads, *kv_loads]:
        copy.wait()

    lane = lax.broadcasted_iota(jnp.int32, (SPAN, HEAD), 1)

    def slots(h, d, i):
        base = lax.rem(a + OFFSET[i] + SIDE, SIDE) * CAP
        spots = [base + k for k in range(CAP)]
        values, scores = [], []
        for at in spots:
            query = qs[d][h][tab_s[d, b, at]]
            cached = tab_s[d, b, 16 + at]
            values.append(kvs[i][h][cached, 1])
            scores.append(
                lax.dot_general(
                    query,
                    kvs[i][h][cached, 0],
                    (((1,), (1,)), ((), ())),
                    preferred_element_type=F32,
                )
                * SCORE
            )
        highest = [jnp.max(score, axis=1, keepdims=True) for score in scores]
        expon = [jnp.exp2(score - high) for score, high in zip(scores, highest)]
        totals = [jnp.sum(one, axis=1, keepdims=True) for one in expon]
        for at, one, value, high, whole in zip(spots, expon, values, highest, totals):
            part = jnp.dot(one.astype(BF16), value, preferred_element_type=F32)
            parts[h % 2, d, at] = part * (1.0 / whole)
            lses[h % 2, d, at] = jnp.broadcast_to(high + jnp.log2(whole), (SPAN, HEAD))

    def merged(sources):
        top = functools.reduce(jnp.maximum, [lse for lse, _ in sources])
        shares = [jnp.exp2(lse - top) for lse, _ in sources]
        whole = functools.reduce(jnp.add, shares)
        mixed = functools.reduce(
            jnp.add, [share * part.astype(F32) for share, (_, part) in zip(shares, sources)]
        )
        return mixed * (1.0 / whole), top + jnp.log2(whole)

    def from_slots(h, d, g):
        found = []
        for n in range(2):
            at = tab_s[d, b, 32 + 2 * g + n]
            used = tab_s[d, b, 64 + 2 * g + n]
            lse = jnp.where(jnp.full((SPAN, HEAD), used, jnp.int32) > 0, lses[h % 2, d, at], FAR)
            found.append((lse, parts[h % 2, d, at]))
        return found

    def stats_of(held, g):
        turned = pltpu.roll(held, lax.rem(HEAD - g, HEAD), 1)
        return jnp.broadcast_to(turned[:, 0:1], (SPAN, HEAD))

    def contribute(h, d, first, last, extra, held):
        def one(g, held):
            sources = from_slots(h, d, g)
            if extra is not None:
                sources.append((stats_of(opp_stats[h, extra], g), opp[h, extra, g - first]))
            mixed, lse = merged(sources)
            sent[h, d - 1, g] = mixed.astype(BF16)
            return jnp.where(lane == g, lse, held)

        return lax.fori_loop(first, last, one, held, unroll=4)

    none = jnp.zeros((SPAN, HEAD), F32)
    opp_copies = [
        [
            remote(sent.at[h, 2, lo_g], opp.at[h, 0], r_sem, (h, 0), along_b(1)),
            remote(stats.at[h, 2], opp_stats.at[h, 0], r_sem, (h, 1), along_b(1)),
            remote(sent.at[h, 2, hi_g], opp.at[h, 1], r_sem, (h, 2), along_b(-1)),
            remote(stats.at[h, 2], opp_stats.at[h, 1], r_sem, (h, 3), along_b(-1)),
        ]
        for h in range(HEADS)
    ]
    back_copies = [
        [
            remote(sent.at[h, 1, hi_g], back.at[h, 0, hi_g], r_sem, (h, 4), along_b(1)),
            remote(sent.at[h, 1, lo_g], back.at[h, 0, lo_g], r_sem, (h, 5), along_b(1)),
            remote(stats.at[h, 1], back_stats.at[h, 0], r_sem, (h, 6), along_b(1)),
            remote(sent.at[h, 0, lo_g], back.at[h, 1, lo_g], r_sem, (h, 7), along_b(-1)),
            remote(sent.at[h, 0, hi_g], back.at[h, 1, hi_g], r_sem, (h, 8), along_b(-1)),
            remote(stats.at[h, 0], back_stats.at[h, 1], r_sem, (h, 9), along_b(-1)),
        ]
        for h in range(HEADS)
    ]
    carry_copies = [
        remote(carried.at[0, h], carried.at[1, h], c_sem, (h,), next_block) for h in range(HEADS)
    ]
    before, after = lax.rem(z + 3, SIDE), lax.rem(z + 1, SIDE)
    ctx_copies = [
        [
            remote(ctx.at[h, z], ctx.at[h, z], x_sem, (h, 0), along_z(1)),
            remote(ctx.at[h, z], ctx.at[h, z], x_sem, (h, 1), along_z(-1)),
            remote(ctx.at[h, before, lo_g], ctx.at[h, before, lo_g], x_sem, (h, 2), along_z(1)),
            remote(ctx.at[h, after, hi_g], ctx.at[h, after, hi_g], x_sem, (h, 3), along_z(-1)),
        ]
        for h in range(HEADS)
    ]

    def pass_on(h):
        arrive(kv_copies[h][0])
        send(kv_copies[h][4])
        arrive(kv_copies[h][1])
        send(kv_copies[h][5])
        arrive(q_copies[h][0])
        send(q_copies[h][4])
        arrive(q_copies[h][1])
        send(q_copies[h][5])
        if h + 2 < HEADS:
            for copy in kv_copies[h + 2][:4] + q_copies[h + 2][:4]:
                send(copy)
        arrive(*kv_copies[h][2:4], *q_copies[h][2:4])

    def finish(h, g):
        sources = from_slots(h, 0, g)
        sources.append((stats_of(back_stats[h, 0], g), back[h, 0, g]))
        sources.append((stats_of(back_stats[h, 1], g), back[h, 1, g]))
        return merged(sources)[0]

    def early(h):
        for d in range(3):
            for i in range(3):
                slots(h, d, i)

    def late(h):
        arrive(*q_copies[h][4:6])
        for i in range(3):
            slots(h, 3, i)
        arrive(*kv_copies[h][4:6])
        slots(h, 3, 3)
        stats[h, 2] = contribute(h, 3, 0, GROUPS, None, none)
        for copy in opp_copies[h]:
            send(copy)
        slots(h, 2, 3)
        held_next = contribute(h, 2, 8, GROUPS, None, none)
        send(back_copies[h][0])
        slots(h, 1, 3)
        held_last = contribute(h, 1, 0, 8, None, none)
        send(back_copies[h][3])
        slots(h, 0, 3)
        return held_next, held_last

    def give_back(h, held_next, held_last):
        arrive(*opp_copies[h][0:2])
        stats[h, 1] = contribute(h, 2, 0, 8, 0, held_next)
        send(back_copies[h][1])
        send(back_copies[h][2])
        arrive(*opp_copies[h][2:4])
        stats[h, 0] = contribute(h, 1, 8, GROUPS, 1, held_last)
        send(back_copies[h][4])
        send(back_copies[h][5])

    head_rows = {}

    def context(h):
        arrive(*back_copies[h])
        mixed = finish(h, GROUPS - 1)
        carried[0, h] = pltpu.roll(mixed, SPAN - 1, 0).astype(BF16)
        send(carry_copies[h])

        def one_span(step, head_row):
            g = GROUPS - 2 - step
            mixed = finish(h, g)
            moved = jnp.where(span_row == SPAN - 1, head_row, pltpu.roll(mixed, SPAN - 1, 0))
            ctx[h, z, g + 1] = moved.astype(BF16)
            return mixed[0:1]

        head_rows[h] = lax.fori_loop(0, GROUPS - 1, one_span, mixed[0:1], unroll=5)

    def context_out(h):
        arrive(carry_copies[h])
        here = jnp.full((SPAN, HEAD), seq, jnp.int32) > 0
        arrived = jnp.where(here, carried[1, h].astype(F32), 0.0)
        ctx[h, z, 0] = jnp.where(span_row == SPAN - 1, head_rows[h], arrived).astype(BF16)
        send(ctx_copies[h][0])
        send(ctx_copies[h][1])

    def context_on(h):
        arrive(ctx_copies[h][0])
        send(ctx_copies[h][2])
        arrive(ctx_copies[h][1])
        send(ctx_copies[h][3])

    def product(h, at, n):
        left = jnp.concatenate([ctx[h, j, at].reshape(-1, HEAD) for j in range(SIDE)], axis=1)
        cut = pl.ds(pl.multiple_of(n * 256, 256), 256)
        right = jnp.concatenate(
            [w_all[j, h * HEAD : (h + 1) * HEAD, cut] for j in range(SIDE)], axis=0
        )
        return jnp.dot(left, right, preferred_element_type=F32), cut

    def project(h):
        if h == 0:
            w_load.wait()
            arrive(*w_copies)
        arrive(*ctx_copies[h][2:4])

        def one(step, carry):
            at = pl.ds((step // 4) * 4, 4)
            value, cut = product(h, at, step % 4)
            value = value.reshape(4, SPAN, 256)
            total[at, :, cut] = value if h == 0 else total[at, :, cut] + value
            return carry

        lax.fori_loop(0, 16, one, 0)

    pass_on(0)
    held = [None] * HEADS
    for h in range(HEADS):
        early(h)
        if h + 1 < HEADS:
            pass_on(h + 1)
        if h >= 1:
            give_back(h - 1, *held[h - 1])
        if h >= 2:
            context_out(h - 2)
        held[h] = late(h)
        if h >= 1:
            context(h - 1)
        if h >= 2:
            context_on(h - 2)
        if h >= 3:
            project(h - 3)
    h = HEADS - 1
    give_back(h, *held[h])
    context_out(h - 1)
    project(h - 2)
    context(h)
    context_on(h - 1)
    context_out(h)
    project(h - 1)
    context_on(h)
    arrive(*ctx_copies[h][2:4])

    ways = (2, 1, -1, 0)
    give_copies = [
        remote(give.at[j], got.at[j], g_sem, (j,), sibling) for j in range(SIDE)
    ]
    ship_copies = [
        remote(ship.at[j], landed.at[j], s_sem, (j,), along_z(by)) for j, by in enumerate(ways[:3])
    ]
    for j, by in enumerate(ways):
        first = lax.rem(z + by + SIDE, SIDE) * 4
        for whose, to in ((1 - core, give), (core, keep)):
            at = pl.ds(first + 2 * whose, 2)

            def one(n, carry, at=at, to=to, j=j):
                value, cut = product(h, at, n)
                value = value + total[at, :, cut].reshape(128, 256)
                to[j, :, cut] = value.astype(to.dtype)
                return carry

            lax.fori_loop(0, 4, one, 0)
            if to is give:
                send(give_copies[j])
    for j, by in enumerate(ways):
        arrive(give_copies[j])
        value = (keep[j] + got[j].astype(F32)).astype(BF16)
        if by == 0:
            out[:, columns(z)] = value
        else:
            ship[j] = value
            send(ship_copies[j])
    for j in (1, 2, 0):
        arrive(ship_copies[j])
        out[:, columns(lax.rem(z - ways[j] + SIDE, SIDE))] = landed[j]
    for copy in started:
        copy.wait_send()


def shards(hidden, query_weight, out_weight, kv_cache, nbr_shard, nbr_row, nbr_count):
    dma = pltpu.SemaphoreType.DMA
    hbm = pl.BlockSpec(memory_space=pl.ANY)
    return pl.pallas_call(
        kernel,
        out_shape=jax.ShapeDtypeStruct((128, 4096), BF16),
        in_specs=[hbm] * 4 + [pl.BlockSpec(memory_space=pltpu.SMEM)] * 3,
        out_specs=pl.BlockSpec(memory_space=pltpu.VMEM),
        scratch_shapes=[
            pltpu.VMEM((4, 256, 4096), BF16),
            pltpu.VMEM((4096, WIDTH), BF16),
            pltpu.VMEM((SIDE, WIDTH, 1024), BF16),
            [[pltpu.VMEM((8, 2, 128, HEAD), BF16)] * HEADS] * SIDE,
            [[pltpu.VMEM((GROUPS, SPAN, HEAD), BF16)] * HEADS] * SIDE,
            pltpu.VMEM((2, SIDE, 16, SPAN, HEAD), F32),
            pltpu.VMEM((2, SIDE, 16, SPAN, HEAD), F32),
            pltpu.VMEM((8, 128), jnp.int32),
            pltpu.VMEM((3, 8, 128), jnp.int32),
            pltpu.SMEM((4, 8, 128), jnp.int32),
            pltpu.VMEM((2, SPAN, WIDTH), BF16),
            pltpu.VMEM((HEADS, 3, GROUPS, SPAN, HEAD), BF16),
            pltpu.VMEM((HEADS, 3, SPAN, HEAD), F32),
            pltpu.VMEM((HEADS, 2, 8, SPAN, HEAD), BF16),
            pltpu.VMEM((HEADS, 2, SPAN, HEAD), F32),
            pltpu.VMEM((HEADS, 2, GROUPS, SPAN, HEAD), BF16),
            pltpu.VMEM((HEADS, 2, SPAN, HEAD), F32),
            pltpu.VMEM((HEADS, SIDE, GROUPS, SPAN, HEAD), BF16),
            pltpu.VMEM((2, HEADS, SPAN, HEAD), BF16),
            pltpu.VMEM((GROUPS, SPAN, 1024), F32),
            pltpu.VMEM((SIDE, 128, 1024), F32),
            pltpu.VMEM((SIDE, 128, 1024), BF16),
            pltpu.VMEM((SIDE, 128, 1024), BF16),
            pltpu.VMEM((3, 128, 1024), BF16),
            pltpu.VMEM((3, 128, 1024), BF16),
            dma((4,)),
            dma((6,)),
            dma((4,)),
            dma((2, HEADS, 6)),
            dma((2, HEADS, 6)),
            dma((2, 3)),
            dma((2,)),
            dma((2, HEADS)),
            dma((2, 3)),
            dma((2, HEADS, 10)),
            dma((2, HEADS, 4)),
            dma((2, SIDE)),
            dma((2, 3)),
        ],
        compiler_params=pltpu.CompilerParams(
            collective_id=0, has_side_effects=True, vmem_limit_bytes=62 * 1024 * 1024
        ),
        cost_estimate=pl.CostEstimate(flops=9_000_000_000, bytes_accessed=20_000_000, transcendentals=2_000_000),
    )(hidden, query_weight, out_weight, kv_cache, nbr_shard.T, nbr_row.T, nbr_count)


def solution(mesh):
    placed = (
        P("seq", None),
        P(None, "tp"),
        P("tp", None),
        P("seq", None, None, "tp"),
        P("seq", None),
        P("seq", None),
        P("seq"),
    )
    return jax.shard_map(
        shards, mesh=mesh, in_specs=placed, out_specs=P(("seq", "tp"), None), check_vma=False
    )
```

time: 408 us -> 141 us (0.35)
  waiting for transfers between devices: 291 us -> 0 us
  Pallas kernels: 0 us -> 138 us
  local copies, waits for them, and re-layouts: 48.8 us -> 2.29 us
  matrix products: 23.3 us -> 0 us
  blocking collectives: 13.8 us -> 0 us
  between operations: 13.6 us -> 0.01 us
  other arithmetic: 8.52 us -> 0 us
  starting transfers between devices: 8.09 us -> 0 us
    ppermute x2 -> x0, waiting for transfers between devices: 232 us -> none  [passed_along(): return lax.ppermute(shard, axis, pairs)]
    pallas_call x0 -> x1, Pallas kernels: none -> 138 us  [shards(): pl.pallas_call(kernel, out_shape=jax.ShapeDtypeStruct((128, 4096), BF16),...]
    reduce_scatter x1 -> x0, waiting for transfers between devices: 59.3 us -> none  [shards(): lax.psum_scatter(jnp.dot(context, out_weight, preferred_element_type=jnp....]
    dot_general x4 -> x0, matrix products: 23.3 us -> none  [the longest x1 7.17 us: shards(): jnp.dot(normed, query_weight, preferred_element_type=jnp.float32)]
    slice x7 -> x0, local copies, waits for them, and re-layouts: 19 us -> none  [the longest x2 12.3 us: attend_spans(): gathered[:, 1]]
    gather x2 -> x0, local copies, waits for them, and re-layouts: 18.3 us -> none  [the longest x1 10.9 us: shards(): gathered = returned[owners, slot_rank]]
    all_to_all x1 -> x0, blocking collectives: 13.8 us -> none  [shards(): lax.all_to_all(asked, 'seq', split_axis=0, concat_axis=0, tiled=True)]
    reduce_sum x4 -> x0, other arithmetic: 7.98 us -> none  [the longest x1 5.22 us: shards(): meansq = jnp.mean(widened * widened, axis=1, keepdims=True)]
  transfers between devices with their start and end apart: 4 -> 0, of which waited for: 3 -> 0; matrix products, arithmetic and copies ran while one was open for 4% -> 0% of each run, Pallas kernels for 0% -> 0%
where the time goes in v2:
time: 141 us
  Pallas kernels  138 us (98%)
  local copies, waits for them, and re-layouts  2.29 us (2%)
    pallas_call x1, Pallas kernels, shards(): pl.pallas_call(kernel, out_shape=jax.ShapeDtypeStruct((128, 4096), BF16),...  138 us

profile of v2, /device:TPU:1, one launch (start us, length us, event | category | flops | bytes accessed | tf_op | source)
XLA Modules:
  0.0 140.7 jit_solution(10991712234501520494)
XLA Ops:
  0.0 138.4 %shard_map.73 = bf16[128,4096]{1,0:T(8,128)(2,1)} custom-call(bf16[1024,4096]{1,0:T(8,128)(2,1)} %hidden.1, bf16[4096,512]{1,0:T(8,128)(2,1)} %wq.1, bf16[512,4096]{1,0:T(8,128)(2,1)} %wo.1, bf16[8,2,128,512]{3,2,1,0:T(8,128)(2,1)} %kv.1, s32[2,16]{1,0:T(2,128)} %bitcast.2, s32[2,16]{1,0:T(2,128)} %bitcast.3, s32[16]{0:T(128)} %count_of.1), custom_call_target="tpu_custom_call" | custom-call | flops 8999999488 | bytes 20000000 | tf_op jit(solution)/shard_map/pallas_call | solution.py:496
  138.4 2.3 %copy.9 = bf16[128,4096]{1,0:T(8,128)(2,1)} copy(bf16[128,4096]{1,0:T(8,128)(2,1)} %shard_map.73) | data formatting | bytes 2097152

commit v3 on v2

--- a/solution.py
+++ b/solution.py
@@ -311,10 +311,12 @@
     before, after = lax.rem(z + 3, SIDE), lax.rem(z + 1, SIDE)
     ctx_copies = [
         [
-            remote(ctx.at[h, z], ctx.at[h, z], x_sem, (h, 0), along_z(1)),
-            remote(ctx.at[h, z], ctx.at[h, z], x_sem, (h, 1), along_z(-1)),
-            remote(ctx.at[h, before, lo_g], ctx.at[h, before, lo_g], x_sem, (h, 2), along_z(1)),
-            remote(ctx.at[h, after, hi_g], ctx.at[h, after, hi_g], x_sem, (h, 3), along_z(-1)),
+            remote(ctx.at[h, z, hi_g], ctx.at[h, z, hi_g], x_sem, (h, 0), along_z(-1)),
+            remote(ctx.at[h, z, hi_g], ctx.at[h, z, hi_g], x_sem, (h, 1), along_z(1)),
+            remote(ctx.at[h, z, lo_g], ctx.at[h, z, lo_g], x_sem, (h, 2), along_z(1)),
+            remote(ctx.at[h, z, lo_g], ctx.at[h, z, lo_g], x_sem, (h, 3), along_z(-1)),
+            remote(ctx.at[h, after, hi_g], ctx.at[h, after, hi_g], x_sem, (h, 4), along_z(-1)),
+            remote(ctx.at[h, before, lo_g], ctx.at[h, before, lo_g], x_sem, (h, 5), along_z(1)),
         ]
         for h in range(HEADS)
     ]
@@ -387,27 +389,30 @@
             ctx[h, z, g + 1] = moved.astype(BF16)
             return mixed[0:1]
 
-        head_rows[h] = lax.fori_loop(0, GROUPS - 1, one_span, mixed[0:1], unroll=5)
+        head_row = lax.fori_loop(0, 8, one_span, mixed[0:1], unroll=4)
+        send(ctx_copies[h][0])
+        send(ctx_copies[h][1])
+        head_rows[h] = lax.fori_loop(8, GROUPS - 1, one_span, head_row, unroll=7)
 
     def context_out(h):
         arrive(carry_copies[h])
         here = jnp.full((SPAN, HEAD), seq, jnp.int32) > 0
         arrived = jnp.where(here, carried[1, h].astype(F32), 0.0)
         ctx[h, z, 0] = jnp.where(span_row == SPAN - 1, head_rows[h], arrived).astype(BF16)
-        send(ctx_copies[h][0])
-        send(ctx_copies[h][1])
+        send(ctx_copies[h][2])
+        send(ctx_copies[h][3])
 
     def context_on(h):
         arrive(ctx_copies[h][0])
-        send(ctx_copies[h][2])
-        arrive(ctx_copies[h][1])
-        send(ctx_copies[h][3])
-
-    def product(h, at, n):
-        left = jnp.concatenate([ctx[h, j, at].reshape(-1, HEAD) for j in range(SIDE)], axis=1)
+        send(ctx_copies[h][4])
+        arrive(ctx_copies[h][2])
+        send(ctx_copies[h][5])
+
+    def product(h, at, n, chips):
+        left = jnp.concatenate([ctx[h, j, at].reshape(-1, HEAD) for j in chips], axis=1)
         cut = pl.ds(pl.multiple_of(n * 256, 256), 256)
         right = jnp.concatenate(
-            [w_all[j, h * HEAD : (h + 1) * HEAD, cut] for j in range(SIDE)], axis=0
+            [w_all[j, h * HEAD : (h + 1) * HEAD, cut] for j in chips], axis=0
         )
         return jnp.dot(left, right, preferred_element_type=F32), cut
 
@@ -415,11 +420,15 @@
         if h == 0:
             w_load.wait()
             arrive(*w_copies)
-        arrive(*ctx_copies[h][2:4])
+        arrive(ctx_copies[h][1], ctx_copies[h][3])
+        chips = (z, before, after)
+        if h + 1 < HEADS:
+            arrive(*ctx_copies[h][4:])
+            chips = range(SIDE)
 
         def one(step, carry):
             at = pl.ds((step // 4) * 4, 4)
-            value, cut = product(h, at, step % 4)
+            value, cut = product(h, at, step % 4, chips)
             value = value.reshape(4, SPAN, 256)
             total[at, :, cut] = value if h == 0 else total[at, :, cut] + value
             return carry
@@ -452,7 +461,8 @@
     context_out(h)
     project(h - 1)
     context_on(h)
-    arrive(*ctx_copies[h][2:4])
+    project(h)
+    arrive(*ctx_copies[h][4:])
 
     ways = (2, 1, -1, 0)
     give_copies = [
@@ -467,7 +477,7 @@
             at = pl.ds(first + 2 * whose, 2)
 
             def one(n, carry, at=at, to=to, j=j):
-                value, cut = product(h, at, n)
+                value, cut = product(h, at, n, (lax.rem(z + 2, SIDE),))
                 value = value + total[at, :, cut].reshape(128, 256)
                 to[j, :, cut] = value.astype(to.dtype)
                 return carry
@@ -483,10 +493,12 @@
         else:
             ship[j] = value
             send(ship_copies[j])
+    for copy in started[:-3]:
+        copy.wait_send()
     for j in (1, 2, 0):
         arrive(ship_copies[j])
         out[:, columns(lax.rem(z - ways[j] + SIDE, SIDE))] = landed[j]
-    for copy in started:
+    for copy in started[-3:]:
         copy.wait_send()
 
 
@@ -534,7 +546,7 @@
             dma((2, HEADS)),
             dma((2, 3)),
             dma((2, HEADS, 10)),
-            dma((2, HEADS, 4)),
+            dma((2, HEADS, 6)),
             dma((2, SIDE)),
             dma((2, 3)),
         ],

time: 141 us -> 137 us (0.972)
  Pallas kernels: 138 us -> 134 us
    pallas_call x1, Pallas kernels: 138 us -> 134 us  [shards(): pl.pallas_call(kernel, out_shape=jax.ShapeDtypeStruct((128, 4096), BF16),...]
where the time goes in v3:
time: 137 us
  Pallas kernels  134 us (98%)
  local copies, waits for them, and re-layouts  2.29 us (2%)
    pallas_call x1, Pallas kernels, shards(): pl.pallas_call(kernel, out_shape=jax.ShapeDtypeStruct((128, 4096), BF16),...  134 us

profile of v3, /device:TPU:1, one launch (start us, length us, event | category | flops | bytes accessed | tf_op | source)
XLA Modules:
  0.0 136.6 jit_solution(3875556378354028534)
XLA Ops:
  0.0 134.3 %shard_map.73 = bf16[128,4096]{1,0:T(8,128)(2,1)} custom-call(bf16[1024,4096]{1,0:T(8,128)(2,1)} %hidden.1, bf16[4096,512]{1,0:T(8,128)(2,1)} %wq.1, bf16[512,4096]{1,0:T(8,128)(2,1)} %wo.1, bf16[8,2,128,512]{3,2,1,0:T(8,128)(2,1)} %kv.1, s32[2,16]{1,0:T(2,128)} %bitcast.2, s32[2,16]{1,0:T(2,128)} %bitcast.3, s32[16]{0:T(128)} %count_of.1), custom_call_target="tpu_custom_call" | custom-call | flops 8999999488 | bytes 20000000 | tf_op jit(solution)/shard_map/pallas_call | solution.py:508
  134.3 2.3 %copy.9 = bf16[128,4096]{1,0:T(8,128)(2,1)} copy(bf16[128,4096]{1,0:T(8,128)(2,1)} %shard_map.73) | data formatting | bytes 2097152

commit v4 on v3

--- a/solution.py
+++ b/solution.py
@@ -199,6 +199,9 @@
                 qs[0][h][0:3] = moved[1:4, :, cut]
             else:
                 qs[0][h][4 * c - 1 : 4 * c + 3] = moved[:, :, cut]
+        if c == 1:
+            arrive(tab_copies[0])
+            send(tab_copies[2])
         if c == 2:
             send(q_copies[0][0])
             send(q_copies[0][3])
@@ -212,17 +215,6 @@
     send(q_copies[0][2])
     for copy in q_copies[1][:4]:
         send(copy)
-
-    arrive(tab_copies[0])
-    send(tab_copies[2])
-    arrive(tab_copies[1], tab_copies[2])
-    tab_loads = [
-        pltpu.make_async_copy(tab_v.at[d], tab_s.at[d + 1], tab_sem.at[d + 1]) for d in range(3)
-    ]
-    for copy in tab_loads:
-        copy.start()
-    for copy in [tab_load, *tab_loads, *kv_loads]:
-        copy.wait()
 
     lane = lax.broadcasted_iota(jnp.int32, (SPAN, HEAD), 1)
 
@@ -290,7 +282,7 @@
             remote(sent.at[h, 2, lo_g], opp.at[h, 0], r_sem, (h, 0), along_b(1)),
             remote(stats.at[h, 2], opp_stats.at[h, 0], r_sem, (h, 1), along_b(1)),
             remote(sent.at[h, 2, hi_g], opp.at[h, 1], r_sem, (h, 2), along_b(-1)),
-            remote(stats.at[h, 2], opp_stats.at[h, 1], r_sem, (h, 3), along_b(-1)),
+            remote(stats.at[h, 3], opp_stats.at[h, 1], r_sem, (h, 3), along_b(-1)),
         ]
         for h in range(HEADS)
     ]
@@ -352,9 +344,10 @@
             slots(h, 3, i)
         arrive(*kv_copies[h][4:6])
         slots(h, 3, 3)
-        stats[h, 2] = contribute(h, 3, 0, GROUPS, None, none)
-        for copy in opp_copies[h]:
-            send(copy)
+        for way in range(2):
+            stats[h, 2 + way] = contribute(h, 3, 8 * way, 8 * way + 8, None, none)
+            send(opp_copies[h][2 * way])
+            send(opp_copies[h][2 * way + 1])
         slots(h, 2, 3)
         held_next = contribute(h, 2, 8, GROUPS, None, none)
         send(back_copies[h][0])
@@ -436,6 +429,16 @@
         lax.fori_loop(0, 16, one, 0)
 
     pass_on(0)
+
+    arrive(tab_copies[1], tab_copies[2])
+    tab_loads = [
+        pltpu.make_async_copy(tab_v.at[d], tab_s.at[d + 1], tab_sem.at[d + 1]) for d in range(3)
+    ]
+    for copy in tab_loads:
+        copy.start()
+    for copy in [tab_load, *tab_loads, *kv_loads]:
+        copy.wait()
+
     held = [None] * HEADS
     for h in range(HEADS):
         early(h)
@@ -523,7 +526,7 @@
             pltpu.SMEM((4, 8, 128), jnp.int32),
             pltpu.VMEM((2, SPAN, WIDTH), BF16),
             pltpu.VMEM((HEADS, 3, GROUPS, SPAN, HEAD), BF16),
-            pltpu.VMEM((HEADS, 3, SPAN, HEAD), F32),
+            pltpu.VMEM((HEADS, 4, SPAN, HEAD), F32),
             pltpu.VMEM((HEADS, 2, 8, SPAN, HEAD), BF16),
             pltpu.VMEM((HEADS, 2, SPAN, HEAD), F32),
             pltpu.VMEM((HEADS, 2, GROUPS, SPAN, HEAD), BF16),

time: 137 us -> 133 us (0.971)
  Pallas kernels: 134 us -> 130 us
    pallas_call x1, Pallas kernels: 134 us -> 130 us  [shards(): pl.pallas_call(kernel, out_shape=jax.ShapeDtypeStruct((128, 4096), BF16),...]
where the time goes in v4:
time: 133 us
  Pallas kernels  130 us (98%)
  local copies, waits for them, and re-layouts  2.29 us (2%)
    pallas_call x1, Pallas kernels, shards(): pl.pallas_call(kernel, out_shape=jax.ShapeDtypeStruct((128, 4096), BF16),...  130 us

profile of v4, /device:TPU:1, one launch (start us, length us, event | category | flops | bytes accessed | tf_op | source)
XLA Modules:
  0.0 132.8 jit_solution(2715058799364339429)
XLA Ops:
  0.0 130.5 %shard_map.73 = bf16[128,4096]{1,0:T(8,128)(2,1)} custom-call(bf16[1024,4096]{1,0:T(8,128)(2,1)} %hidden.1, bf16[4096,512]{1,0:T(8,128)(2,1)} %wq.1, bf16[512,4096]{1,0:T(8,128)(2,1)} %wo.1, bf16[8,2,128,512]{3,2,1,0:T(8,128)(2,1)} %kv.1, s32[2,16]{1,0:T(2,128)} %bitcast.2, s32[2,16]{1,0:T(2,128)} %bitcast.3, s32[16]{0:T(128)} %count_of.1), custom_call_target="tpu_custom_call" | custom-call | flops 8999999488 | bytes 20000000 | tf_op jit(solution)/shard_map/pallas_call | solution.py:511
  130.5 2.3 %copy.9 = bf16[128,4096]{1,0:T(8,128)(2,1)} copy(bf16[128,4096]{1,0:T(8,128)(2,1)} %shard_map.73) | data formatting | bytes 2097152
